TPU v7x, 32 devices: a whole 2x2x4 slice. The times are simulated.
32 devices in a mesh: groups: 2 (over y), gy: 16 (over z, x, core).
Axes of the slice: x: 2, y: 2, z: 4, core: 2. Of those that a mesh axis runs over, the one named last changes fastest.
Arguments:
- adjoint: float32 [16, 256, 1024], P('groups', 'gy'), parts along dimension 0, may hold values from -6 to 6
- coeffs: float32 [4, 256, 1024], P(None, 'gy'), may hold values from 0.1 to 0.24
- dist: int32 [256, 1024], P('gy'), may hold values from 0 to 16, as said below
- sources: int32 [2048, 128], P('gy'), may hold values from 0 to 16383, as said below
- weights: bfloat16 [2048, 128, 128], P('gy'), may hold values from -0.5 to 0.5
- owners: int32 [2048, 1], P('gy'), may hold values from 0 to 15; in each aligned block of 128 rows (0 to 127, 128 to 255, ...) at most 16 rows name the same one
- slots: int32 [2048], P('gy'), may hold values from 0 to 31
- counts: int32 [16], P('gy'), may hold values from 96 to 128, as said below
Outputs:
- grad_state: float32 [16, 256, 1024], P('groups', 'gy'), parts along dimension 0
- host_adjoint: float32 [512, 16, 128], P('gy', 'groups'), parts along dimension 1
There are 2 independent parts, one for each index of `groups`. A program takes and returns all parts, laid end to end along the dimension named above; an argument that names none is the same for every part. Nothing has to cross between parts.
Inputs may be any that keep to these rules, and one draw needn't show every extreme that they name: `owners`: within the 128 blocks of one device at most 16 name one owner, a bound that some block reaches. `counts`: a device's blocks b with b < its count are live, the rest padding; the first and last device have 128 live blocks. `sources`: each entry is row * 1024 + column of a cell of the device's own rows, within 16 columns of the left or right edge. `dist`: a cell's distance to the grid's edge plus 0 to 2, capped at 16.
All inputs are finite; a program needn't handle non-finite values.
Results may differ from a plain program's by a relative error of at most 0.0029.
Values sent between devices are 32-bit elements; how exact they have to be, the bound alone decides.
A program may use at most 64 MiB of HBM per device.

v0:
```python
import jax
import jax.numpy as jnp
from jax import lax
from jax.sharding import PartitionSpec as P

ZW = 16
SUB = 4
HOST_BLK = 32


def from_behind(value, axis, steps):
    count = lax.axis_size(axis)
    initial, last = (max(0, -steps), min(count, count - steps))
    return lax.ppermute(value, axis, [(source, source + steps) for source in range(initial, last)])


def davies(dist):
    frac = 1.0 - dist.astype(jnp.float32) / ZW
    return frac * frac


def sideways(field, k_west, k_east):
    g_west = k_west * field
    g_east = k_east * field
    zero_col = jnp.zeros_like(field[:, :, :1])
    left_part = jnp.concatenate([g_west[:, :, 1:], zero_col], 2)
    right_part = jnp.concatenate([zero_col, g_east[:, :, :-1]], 2)
    return (left_part, right_part)


def local(adjoint, coeffs, dist, sources, weights, owners, slots, counts):
    levels, rows, width = adjoint.shape
    nblk = sources.shape[0]
    host_width = weights.shape[2]
    owner_count = lax.axis_size("gy")
    capacity = max(2, (2 * nblk + owner_count - 1) // owner_count)
    relax = davies(dist)
    k_north, k_south, k_west, k_east = (coeffs[0], coeffs[1], coeffs[2], coeffs[3])
    total = k_north + k_south + k_west + k_east
    zone = (relax * adjoint).reshape(levels, rows * width)
    values = jnp.take(zone, sources, axis=1).astype(jnp.bfloat16)
    contrib = jnp.einsum("lbk,bkh->blh", values, weights, preferred_element_type=jnp.float32)
    live = lax.iota(jnp.int32, nblk) < counts[0]
    flat_contrib = jnp.where(live[:, None, None], contrib, 0.0).reshape(nblk, levels * host_width)
    owner_ids = owners[:, 0]
    onehot = (owner_ids[:, None] == lax.iota(jnp.int32, owner_count)[None, :]).astype(jnp.int32)
    before = jnp.cumsum(onehot, axis=0) - onehot
    position = jnp.sum(before * onehot, axis=1)
    target = owner_ids * capacity + position
    packed = (
        jnp.zeros((owner_count * capacity, levels * host_width), jnp.float32)
        .at[target]
        .set(flat_contrib)
    )
    block_ids = (
        jnp.full((owner_count * capacity,), -1.0, jnp.float32)
        .at[target]
        .set(jnp.where(live, slots.astype(jnp.float32), -1.0))
    )
    received, got_ids = (
        lax.all_to_all(
            packed.reshape(owner_count, capacity, levels * host_width),
            "gy",
            split_axis=0,
            concat_axis=0,
            tiled=True,
        ),
        lax.all_to_all(
            block_ids.reshape(owner_count, capacity), "gy", split_axis=0, concat_axis=0, tiled=True
        ),
    )
    flat_ids = got_ids.reshape(-1).astype(jnp.int32)
    flat_ids = jnp.where(flat_ids >= 0, flat_ids, HOST_BLK)
    buffer = jnp.zeros((HOST_BLK + 1, levels * host_width), jnp.float32)
    host = buffer.at[flat_ids].add(received.reshape(owner_count * capacity, levels * host_width))[
        :HOST_BLK
    ]
    host_adjoint = host.reshape(HOST_BLK, levels, host_width)
    field = (1.0 - relax) * adjoint
    for step in range(SUB):
        g_north = k_north * field
        g_south = k_south * field
        below = from_behind(g_north[:, :1, :], "gy", -1)
        above = from_behind(g_south[:, -1:, :], "gy", 1)
        upper = jnp.concatenate([g_north[:, 1:, :], below], 1)
        lower = jnp.concatenate([above, g_south[:, :-1, :]], 1)
        left_part, right_part = sideways(field, k_west, k_east)
        field = field * (1.0 - total) + upper + lower + left_part + right_part
    return (field, host_adjoint)


def solution(mesh):
    placed = (
        P("groups", "gy", None),
        P(None, "gy", None),
        P("gy", None),
        P("gy", None),
        P("gy", None, None),
        P("gy", None),
        P("gy"),
        P("gy"),
    )
    return jax.shard_map(
        local,
        mesh=mesh,
        in_specs=placed,
        out_specs=(P("groups", "gy", None), P("gy", "groups", None)),
        check_vma=False,
    )
```

profile of v0, /device:TPU:16, one launch (start us, length us, event | category | flops | bytes accessed | tf_op | source)
XLA Modules:
  0.0 148.8 jit_solution(10374053487806515872)
XLA Ops:
  0.7 1.0 subtract_bitcast_fusion
  2.5 1.2 broadcast_multiply_fusion.4
  4.4 2.7 %collective-permute-start = (f32[8,1,1024]{2,1,0:T(1,128)}, f32[8,1,1024]{2,1,0:T(1,128)S(1)}, u32[]{:S(2)}, u32[]{:S(2)}) collective-permute-start(f32[8,1,1024]{2,1,0:T(1,128)} %slice.119), channel_id=1, source_target_pairs={{1,0},{2,1},{3,2},{4,3},{5,4},{6,5},{7,6},{8,7},{9,8},{10,9},{11,1... | collective-permute-start | bytes 98312 | tf_op jit(solution)/shard_map/ppermute | solution.py:14
  7.7 1.9 %collective-permute-start.1 = (f32[8,1,1024]{2,1,0:T(1,128)}, f32[8,1,1024]{2,1,0:T(1,128)S(1)}, u32[]{:S(2)}, u32[]{:S(2)}) collective-permute-start(f32[8,1,1024]{2,1,0:T(1,128)} %slice.120), channel_id=1, source_target_pairs={{0,1},{1,2},{2,3},{3,4},{4,5},{5,6},{6,7},{7,8},{8,9},{9,10},{10,1... | collective-permute-start | bytes 98312 | tf_op jit(solution)/shard_map/ppermute | solution.py:14
  15.1 6.4 %all-to-all-start = ((f32[16,1,16]{2,1,0:T(1,128)}), f32[16,1,16]{2,1,0:T(1,128)S(1)}, u32[]{:S(2)}, u32[]{:S(2)}) async-start(f32[16,1,16]{2,1,0:T(1,128)} %all_to_all.9), calls=%async_computation | async-start | bytes 16384 | tf_op jit(solution)/shard_map/all_to_all | solution.py:68
  22.5 3.1 %copy.10 = bf16[8,16,1024]{0,2,1:T(8,128)(2,1)} copy(bf16[8,16,1024]{2,1,0:T(8,128)(2,1)S(1)} %broadcast_multiply_fusion) | data formatting | bytes 524288 | tf_op jit(solution)/shard_map/mul | solution.py:40
  25.6 58.1 %gather_fusion = bf16[16384,8]{1,0:T(8,128)(2,1)} fusion(bf16[8,16384]{0,1:T(8,128)(2,1)} %bitcast.43, s32[16384]{0:T(1024)S(1)} %bitcast_clamp_fusion), kind=kCustom, calls=%fused_computation | custom fusion | bytes 589824 | tf_op jit(solution)/shard_map/jit(_take)/gather | solution.py:41
  83.7 3.8 %copy.11 = bf16[128,128,8]{1,2,0:T(8,128)(2,1)S(1)} copy(bf16[128,128,8]{2,1,0:T(8,128)(2,1)} %bitcast.44) | data formatting | bytes 524288 | tf_op jit(solution)/shard_map/jit(_take)/gather | solution.py:41
  87.5 3.4 %convolution_select_fusion = f32[128,8,128]{2,1,0:T(8,128)S(1)} fusion(bf16[128,128,128]{2,1,0:T(8,128)(2,1)} %param.12, bf16[128,128,8]{1,2,0:T(8,128)(2,1)S(1)} %copy.11, pred[128]{0:T(512)(128)(4,1)S(1)} %iota_compare_fusion.1, pred[128,128]{1,0:T(8,128)(4,1)S(1)} %compare_and_fusion), kind=kOutput, calls=%fused_computation.4 | convolution fusion | flops 33816576 | bytes 4997248 | tf_op jit(solution)/shard_map/lbk,bkh->blh/dot_general | solution.py:42
  92.0 2.1 %scatter_custom_fusion.1 = f32[256,1024]{1,0:T(8,128)} fusion(s32[128]{0:T(128)S(1)} %fusion.23, f32[16,8,8,128]{3,2,1,0:T(8,128)S(1)} %bitcast.49, f32[]{:T(128)} %constant.14.clone.1), kind=kCustom, calls=%fused_computation.5 | custom fusion | bytes 1572868 | tf_op jit(solution)/shard_map/scatter | solution.py:53
  94.1 6.0 %all-to-all-start.1 = ((f32[16,16,1024]{2,1,0:T(8,128)}), f32[16,16,1024]{2,1,0:T(8,128)}, u32[]{:S(2)}, u32[]{:S(2)}) async-start(f32[16,16,1024]{2,1,0:T(8,128)} %bitcast.14), calls=%async_computation.1 | async-start | bytes 2097152 | tf_op jit(solution)/shard_map/all_to_all | solution.py:61
  100.3 1.4 broadcast_multiply_fusion.3
  101.7 3.1 %collective-permute-start.2 = (f32[8,1,1024]{2,1,0:T(1,128)S(1)}, f32[8,1,1024]{2,1,0:T(1,128)S(1)}, u32[]{:S(2)}, u32[]{:S(2)}) collective-permute-start(f32[8,1,1024]{2,1,0:T(1,128)S(1)} %slice.127), channel_id=1, source_target_pairs={{1,0},{2,1},{3,2},{4,3},{5,4},{6,5},{7,6},{8,7},{9,8},{10,9},{11,1... | collective-permute-start | bytes 98312 | tf_op jit(solution)/shard_map/ppermute | solution.py:14
  104.9 1.9 %collective-permute-start.3 = (f32[8,1,1024]{2,1,0:T(1,128)S(1)}, f32[8,1,1024]{2,1,0:T(1,128)S(1)}, u32[]{:S(2)}, u32[]{:S(2)}) collective-permute-start(f32[8,1,1024]{2,1,0:T(1,128)S(1)} %slice.128), channel_id=1, source_target_pairs={{0,1},{1,2},{2,3},{3,4},{4,5},{5,6},{6,7},{7,8},{8,9},{9,10},{10,1... | collective-permute-start | bytes 98312 | tf_op jit(solution)/shard_map/ppermute | solution.py:14
  107.1 16.6 %collective-permute-done.2 = f32[8,1,1024]{2,1,0:T(1,128)S(1)} collective-permute-done((f32[8,1,1024]{2,1,0:T(1,128)S(1)}, f32[8,1,1024]{2,1,0:T(1,128)S(1)}, u32[]{:S(2)}, u32[]{:S(2)}) %collective-permute-start.2) | collective-permute-done | bytes 32800 | tf_op jit(solution)/shard_map/ppermute | solution.py:14
  123.7 1.8 %collective-permute-done.3 = f32[8,1,1024]{2,1,0:T(1,128)S(1)} collective-permute-done((f32[8,1,1024]{2,1,0:T(1,128)S(1)}, f32[8,1,1024]{2,1,0:T(1,128)S(1)}, u32[]{:S(2)}, u32[]{:S(2)}) %collective-permute-start.3) | collective-permute-done | bytes 32800 | tf_op jit(solution)/shard_map/ppermute | solution.py:14
  126.0 2.9 %collective-permute-start.4 = (f32[8,1,1024]{2,1,0:T(1,128)S(1)}, f32[8,1,1024]{2,1,0:T(1,128)S(1)}, u32[]{:S(2)}, u32[]{:S(2)}) collective-permute-start(f32[8,1,1024]{2,1,0:T(1,128)S(1)} %slice.135), channel_id=1, source_target_pairs={{1,0},{2,1},{3,2},{4,3},{5,4},{6,5},{7,6},{8,7},{9,8},{10,9},{11,1... | collective-permute-start | bytes 98312 | tf_op jit(solution)/shard_map/ppermute | solution.py:14
  128.9 1.9 %collective-permute-start.5 = (f32[8,1,1024]{2,1,0:T(1,128)S(1)}, f32[8,1,1024]{2,1,0:T(1,128)S(1)}, u32[]{:S(2)}, u32[]{:S(2)}) collective-permute-start(f32[8,1,1024]{2,1,0:T(1,128)S(1)} %slice.136), channel_id=1, source_target_pairs={{0,1},{1,2},{2,3},{3,4},{4,5},{5,6},{6,7},{7,8},{8,9},{9,10},{10,1... | collective-permute-start | bytes 98312 | tf_op jit(solution)/shard_map/ppermute | solution.py:14
  131.2 3.9 %collective-permute-done.5 = f32[8,1,1024]{2,1,0:T(1,128)S(1)} collective-permute-done((f32[8,1,1024]{2,1,0:T(1,128)S(1)}, f32[8,1,1024]{2,1,0:T(1,128)S(1)}, u32[]{:S(2)}, u32[]{:S(2)}) %collective-permute-start.5) | collective-permute-done | bytes 32800 | tf_op jit(solution)/shard_map/ppermute | solution.py:14
  135.5 1.9 %collective-permute-start.6 = (f32[8,1,1024]{2,1,0:T(1,128)S(1)}, f32[8,1,1024]{2,1,0:T(1,128)S(1)}, u32[]{:S(2)}, u32[]{:S(2)}) collective-permute-start(f32[8,1,1024]{2,1,0:T(1,128)S(1)} %slice.143), channel_id=1, source_target_pairs={{1,0},{2,1},{3,2},{4,3},{5,4},{6,5},{7,6},{8,7},{9,8},{10,9},{11,1... | collective-permute-start | bytes 98312 | tf_op jit(solution)/shard_map/ppermute | solution.py:14
  137.5 2.4 %collective-permute-start.7 = (f32[8,1,1024]{2,1,0:T(1,128)S(1)}, f32[8,1,1024]{2,1,0:T(1,128)S(1)}, u32[]{:S(2)}, u32[]{:S(2)}) collective-permute-start(f32[8,1,1024]{2,1,0:T(1,128)S(1)} %slice.144), channel_id=1, source_target_pairs={{0,1},{1,2},{2,3},{3,4},{4,5},{5,6},{6,7},{7,8},{8,9},{9,10},{10,1... | collective-permute-start | bytes 98312 | tf_op jit(solution)/shard_map/ppermute | solution.py:14
  140.2 3.4 %collective-permute-done.7 = f32[8,1,1024]{2,1,0:T(1,128)S(1)} collective-permute-done((f32[8,1,1024]{2,1,0:T(1,128)S(1)}, f32[8,1,1024]{2,1,0:T(1,128)S(1)}, u32[]{:S(2)}, u32[]{:S(2)}) %collective-permute-start.7) | collective-permute-done | bytes 32800 | tf_op jit(solution)/shard_map/ppermute | solution.py:14
  143.6 1.1 fusion.14
  144.8 3.3 %scatter_custom_fusion.2 = f32[33,1024]{1,0:T(8,128)S(1)} fusion(s32[256]{0:T(256)S(1)} %bitcast.57, f32[256,1024]{1,0:T(8,128)} %bitcast.15, f32[]{:T(128)} %constant.14.clone.1), kind=kCustom, calls=%fused_computation.49 | custom fusion | flops 262144 | bytes 135680 | tf_op jit(solution)/shard_map/scatter-add | solution.py:75
  (50 shorter events, 11.6 us)
Async XLA Ops:
  0.6 21.8 %copy-start = (f32[8,16,1024]{2,1,0:T(8,128)S(1)}, f32[8,16,1024]{2,1,0:T(8,128)}, u32[]{:S(2)}) copy-start(f32[8,16,1024]{2,1,0:T(8,128)} %param.8) | copy-start | bytes 1572868
  0.6 21.7 %copy-start.1 = (s32[128,128]{1,0:T(8,128)S(1)}, s32[128,128]{1,0:T(8,128)}, u32[]{:S(2)}) copy-start(s32[128,128]{1,0:T(8,128)} %param.11) | copy-start | bytes 196612
  4.4 95.9 %collective-permute-start = (f32[8,1,1024]{2,1,0:T(1,128)}, f32[8,1,1024]{2,1,0:T(1,128)S(1)}, u32[]{:S(2)}, u32[]{:S(2)}) collective-permute-start(f32[8,1,1024]{2,1,0:T(1,128)} %slice.119), channel_id=1, source_target_pairs={{1,0},{2,1},{3,2},{4,3},{5,4},{6,5},{7,6},{8,7},{9,8},{10,9},{11,1... | collective-permute-start | bytes 98312 | tf_op jit(solution)/shard_map/ppermute | solution.py:14
  7.7 92.5 %collective-permute-start.1 = (f32[8,1,1024]{2,1,0:T(1,128)}, f32[8,1,1024]{2,1,0:T(1,128)S(1)}, u32[]{:S(2)}, u32[]{:S(2)}) collective-permute-start(f32[8,1,1024]{2,1,0:T(1,128)} %slice.120), channel_id=1, source_target_pairs={{0,1},{1,2},{2,3},{3,4},{4,5},{5,6},{6,7},{7,8},{8,9},{9,10},{10,1... | collective-permute-start | bytes 98312 | tf_op jit(solution)/shard_map/ppermute | solution.py:14
  15.1 79.0 %all-to-all-start = ((f32[16,1,16]{2,1,0:T(1,128)}), f32[16,1,16]{2,1,0:T(1,128)S(1)}, u32[]{:S(2)}, u32[]{:S(2)}) async-start(f32[16,1,16]{2,1,0:T(1,128)} %all_to_all.9), calls=%async_computation | async-start | bytes 16384 | tf_op jit(solution)/shard_map/all_to_all | solution.py:68
  94.1 50.7 %all-to-all-start.1 = ((f32[16,16,1024]{2,1,0:T(8,128)}), f32[16,16,1024]{2,1,0:T(8,128)}, u32[]{:S(2)}, u32[]{:S(2)}) async-start(f32[16,16,1024]{2,1,0:T(8,128)} %bitcast.14), calls=%async_computation.1 | async-start | bytes 2097152 | tf_op jit(solution)/shard_map/all_to_all | solution.py:61
  101.7 22.0 %collective-permute-start.2 = (f32[8,1,1024]{2,1,0:T(1,128)S(1)}, f32[8,1,1024]{2,1,0:T(1,128)S(1)}, u32[]{:S(2)}, u32[]{:S(2)}) collective-permute-start(f32[8,1,1024]{2,1,0:T(1,128)S(1)} %slice.127), channel_id=1, source_target_pairs={{1,0},{2,1},{3,2},{4,3},{5,4},{6,5},{7,6},{8,7},{9,8},{10,9},{11,1... | collective-permute-start | bytes 98312 | tf_op jit(solution)/shard_map/ppermute | solution.py:14
  104.9 20.6 %collective-permute-start.3 = (f32[8,1,1024]{2,1,0:T(1,128)S(1)}, f32[8,1,1024]{2,1,0:T(1,128)S(1)}, u32[]{:S(2)}, u32[]{:S(2)}) collective-permute-start(f32[8,1,1024]{2,1,0:T(1,128)S(1)} %slice.128), channel_id=1, source_target_pairs={{0,1},{1,2},{2,3},{3,4},{4,5},{5,6},{6,7},{7,8},{8,9},{9,10},{10,1... | collective-permute-start | bytes 98312 | tf_op jit(solution)/shard_map/ppermute | solution.py:14
  126.0 5.2 %collective-permute-start.4 = (f32[8,1,1024]{2,1,0:T(1,128)S(1)}, f32[8,1,1024]{2,1,0:T(1,128)S(1)}, u32[]{:S(2)}, u32[]{:S(2)}) collective-permute-start(f32[8,1,1024]{2,1,0:T(1,128)S(1)} %slice.135), channel_id=1, source_target_pairs={{1,0},{2,1},{3,2},{4,3},{5,4},{6,5},{7,6},{8,7},{9,8},{10,9},{11,1... | collective-permute-start | bytes 98312 | tf_op jit(solution)/shard_map/ppermute | solution.py:14
  128.9 6.1 %collective-permute-start.5 = (f32[8,1,1024]{2,1,0:T(1,128)S(1)}, f32[8,1,1024]{2,1,0:T(1,128)S(1)}, u32[]{:S(2)}, u32[]{:S(2)}) collective-permute-start(f32[8,1,1024]{2,1,0:T(1,128)S(1)} %slice.136), channel_id=1, source_target_pairs={{0,1},{1,2},{2,3},{3,4},{4,5},{5,6},{6,7},{7,8},{8,9},{9,10},{10,1... | collective-permute-start | bytes 98312 | tf_op jit(solution)/shard_map/ppermute | solution.py:14
  135.5 4.7 %collective-permute-start.6 = (f32[8,1,1024]{2,1,0:T(1,128)S(1)}, f32[8,1,1024]{2,1,0:T(1,128)S(1)}, u32[]{:S(2)}, u32[]{:S(2)}) collective-permute-start(f32[8,1,1024]{2,1,0:T(1,128)S(1)} %slice.143), channel_id=1, source_target_pairs={{1,0},{2,1},{3,2},{4,3},{5,4},{6,5},{7,6},{8,7},{9,8},{10,9},{11,1... | collective-permute-start | bytes 98312 | tf_op jit(solution)/shard_map/ppermute | solution.py:14
  137.5 6.1 %collective-permute-start.7 = (f32[8,1,1024]{2,1,0:T(1,128)S(1)}, f32[8,1,1024]{2,1,0:T(1,128)S(1)}, u32[]{:S(2)}, u32[]{:S(2)}) collective-permute-start(f32[8,1,1024]{2,1,0:T(1,128)S(1)} %slice.144), channel_id=1, source_target_pairs={{0,1},{1,2},{2,3},{3,4},{4,5},{5,6},{6,7},{7,8},{8,9},{9,10},{10,1... | collective-permute-start | bytes 98312 | tf_op jit(solution)/shard_map/ppermute | solution.py:14
where the time goes:
time: 150 us; the launch traced here: 149 us
  local copies, waits for them, and re-layouts  72 us (48%)
  starting transfers between devices  31.3 us (21%)
  waiting for transfers between devices  25.8 us (17%)
  other arithmetic  14.7 us (10%)
  matrix products  3.38 us (2%)
  between operations  1.65 us (1%)
    gather x2, local copies, waits for them, and re-layouts, local(): values = jnp.take(zone, sources, axis=1).astype(jnp.bfloat16)  61.9 us
    ppermute x8, waiting for transfers between devices, from_behind(): lax.ppermute(value, axis, [(source, source + steps) for source in range(i...  25.8 us
    ppermute x8, starting transfers between devices, from_behind(): lax.ppermute(value, axis, [(source, source + steps) for source in range(i...  18.8 us
    all_to_all x1, starting transfers between devices, local(): lax.all_to_all(block_ids.reshape(owner_count, capacity), 'gy', split_axis...  6.4 us
    all_to_all x1, starting transfers between devices, local(): lax.all_to_all(packed.reshape(owner_count, capacity, levels * host_width)...  6.04 us
    dot_general x1, matrix products, local(): jnp.einsum('lbk,bkh->blh', values, weights, preferred_element_type=jnp.fl...  3.38 us
    scatter-add x1, other arithmetic, local(): buffer.at[flat_ids]  3.35 us
    mul x4, other arithmetic, local(): g_south = k_south * field  3.24 us
  transfers between devices with their start and end apart: 10, of which 4 were waited for; matrix products, arithmetic and copies ran while one was open for 55% of the time, Pallas kernels for 0%

commit v1 on v0

--- a/solution.py
+++ b/solution.py
@@ -1,11 +1,17 @@
+import functools
+
 import jax
 import jax.numpy as jnp
 from jax import lax
+from jax.experimental import pallas as pl
+from jax.experimental.pallas import tpu as pltpu
 from jax.sharding import PartitionSpec as P
 
 ZW = 16
 SUB = 4
 HOST_BLK = 32
+STEP_BLOCKS = 16
+MESH = pl.DeviceIdType.MESH
 
 
 def from_behind(value, axis, steps):
@@ -28,12 +34,286 @@
     return (left_part, right_part)
 
 
+def split_dot(onehot, x):
+    hi = x.astype(jnp.bfloat16)
+    lo = (x - hi.astype(jnp.float32)).astype(jnp.bfloat16)
+    return jnp.dot(onehot, hi, preferred_element_type=jnp.float32) + jnp.dot(
+        onehot, lo, preferred_element_type=jnp.float32
+    )
+
+
+def contrib_kernel(
+    owner_count, capacity, width, src_ref, w_ref, left_ref, right_ref, dleft_ref, dright_ref,
+    owner_ref, slot_ref, count_ref, packed_ref, table, contrib,
+):
+    step = pl.program_id(0)
+    nblk = owner_ref.shape[1]
+    levels, rows, lanes = left_ref.shape
+    per = lanes // (2 * ZW)
+
+    @pl.when(step == 0)
+    def _():
+        lane = lax.broadcasted_iota(jnp.int32, (levels, lanes), 1)
+        for q in range(rows // per):
+            tile = jnp.zeros((levels, lanes), jnp.float32)
+            for i in range(per):
+                r = q * per + i
+                zl = davies(dleft_ref[r : r + 1, :]) * left_ref[:, r, :]
+                zr = davies(dright_ref[r : r + 1, :]) * right_ref[:, r, :]
+                both = jnp.where(lane < lanes // 2, zl, zr)
+                both = pltpu.roll(both, (ZW + 2 * ZW * i) % lanes, 1)
+                tile = jnp.where(lane // (2 * ZW) == i, both, tile)
+            table[q] = tile
+
+    src = src_ref[...]
+    row = src // width
+    col = src % width
+    spot = jnp.where(col < ZW, col + ZW, col - (width - ZW)) + (row % per) * (2 * ZW)
+    group = row // per
+    for j in range(src.shape[0]):
+        at = jnp.broadcast_to(spot[j : j + 1, :], (levels, lanes))
+        which = jnp.broadcast_to(group[j : j + 1, :], (levels, lanes))
+        value = jnp.take_along_axis(table[0], at, axis=1)
+        for q in range(1, rows // per):
+            value = jnp.where(which == q, jnp.take_along_axis(table[q], at, axis=1), value)
+        out = jnp.dot(value.astype(jnp.bfloat16), w_ref[j], preferred_element_type=jnp.float32)
+        contrib[pl.ds(step * STEP_BLOCKS + j, levels, stride=nblk), :] = out
+
+    @pl.when(step == pl.num_programs(0) - 1)
+    def _():
+        owner = owner_ref[...]
+        names = owner == lax.broadcasted_iota(jnp.int32, (owner_count, nblk), 0)
+        onehot = jnp.where(names, 1.0, 0.0)
+        earlier = lax.broadcasted_iota(jnp.int32, (nblk, nblk), 0) < lax.broadcasted_iota(
+            jnp.int32, (nblk, nblk), 1
+        )
+        before = jnp.dot(
+            onehot.astype(jnp.bfloat16),
+            jnp.where(earlier, 1.0, 0.0).astype(jnp.bfloat16),
+            preferred_element_type=jnp.float32,
+        )
+        rank = jnp.sum(onehot * before, axis=0, keepdims=True).astype(jnp.int32)
+        target = owner * capacity + rank
+        live = lax.broadcasted_iota(jnp.int32, (1, nblk), 1) < count_ref[0]
+        target = jnp.where(live, target, -1)
+        places = owner_count * capacity
+        hit = lax.broadcasted_iota(jnp.int32, (places, nblk), 0) == target
+        place = jnp.where(hit, 1.0, 0.0).astype(jnp.bfloat16)
+        for l in range(levels):
+            packed_ref[l] = split_dot(place, contrib[l * nblk : (l + 1) * nblk, :])
+        ids = jnp.sum(jnp.where(hit, slot_ref[...].astype(jnp.float32), 0.0), axis=1, keepdims=True)
+        packed_ref[levels] = jnp.broadcast_to(ids, (places, packed_ref.shape[2]))
+
+
+def exchange_kernel(
+    n, capacity, packed_ref, adjoint_ref, coeffs_ref, dist_ref, grad_ref, host_ref,
+    field, coef, turned, received, halo_send, halo_recv, own_sem, send_sem, recv_sem,
+):
+    me = lax.axis_index("gy")
+    rows, width = dist_ref.shape
+    levels = adjoint_ref.shape[0] // rows
+    pad = 8
+    barrier = pltpu.get_barrier_semaphore()
+    for k in range(1, n):
+        pl.semaphore_signal(barrier, inc=1, device_id={"gy": lax.rem(me + k, n)}, device_id_type=MESH)
+
+    own = pltpu.make_async_copy(coeffs_ref, coef.at[:, pad : pad + rows, :], own_sem)
+    own.start()
+
+    tiles = width // 128
+    for c in range(tiles):
+        turned[c] = adjoint_ref[:, c * 128 : (c + 1) * 128]
+
+    @pl.loop(0, rows)
+    def _(r):
+        keep = 1.0 - davies(dist_ref[pl.ds(r, 1), :])
+        for c in range(tiles):
+            cut = slice(c * 128, (c + 1) * 128)
+            field[r + SUB, :, cut] = keep[:, cut] * turned[c, pl.ds(r, levels, stride=rows), :]
+
+    pl.semaphore_wait(barrier, n - 1)
+
+    def halo(up):
+        to = {"gy": me - 1 if up else me + 1}
+        at = 0 if up else 1
+        first = SUB if up else rows
+        return [
+            pltpu.make_async_remote_copy(
+                src_ref=field.at[first : first + SUB],
+                dst_ref=field.at[rows + SUB : rows + 2 * SUB] if up else field.at[0:SUB],
+                send_sem=halo_send.at[at, 0],
+                recv_sem=halo_recv.at[at, 0],
+                device_id=to,
+                device_id_type=MESH,
+            ),
+            pltpu.make_async_remote_copy(
+                src_ref=coeffs_ref.at[:, 0:pad, :] if up else coeffs_ref.at[:, rows - pad : rows, :],
+                dst_ref=coef.at[:, rows + pad :, :] if up else coef.at[:, 0:pad, :],
+                send_sem=halo_send.at[at, 1],
+                recv_sem=halo_recv.at[at, 1],
+                device_id=to,
+                device_id_type=MESH,
+            ),
+        ]
+
+    up, down = halo(True), halo(False)
+
+    @pl.when(me > 0)
+    def _():
+        for copy in up:
+            copy.start()
+
+    @pl.when(me < n - 1)
+    def _():
+        for copy in down:
+            copy.start()
+
+    copies = []
+    for k in range(1, n):
+        to = lax.rem(me + k, n)
+        copy = pltpu.make_async_remote_copy(
+            src_ref=packed_ref.at[:, pl.ds(pl.multiple_of(to * capacity, 8), capacity), :],
+            dst_ref=received.at[:, pl.ds(pl.multiple_of(me * capacity, 8), capacity), :],
+            send_sem=send_sem.at[k - 1],
+            recv_sem=recv_sem.at[k - 1],
+            device_id={"gy": to},
+            device_id_type=MESH,
+        )
+        copy.start()
+        copies.append(copy)
+    mine = pl.ds(pl.multiple_of(me * capacity, 8), capacity)
+    received[:, mine, :] = packed_ref[:, mine, :]
+
+    @pl.when(me == 0)
+    def _():
+        field[0:SUB] = jnp.zeros((SUB, levels, width), jnp.float32)
+        coef[:, 0:pad, :] = jnp.zeros((4, pad, width), jnp.float32)
+
+    @pl.when(me == n - 1)
+    def _():
+        field[rows + SUB :] = jnp.zeros((SUB, levels, width), jnp.float32)
+        coef[:, rows + pad :, :] = jnp.zeros((4, pad, width), jnp.float32)
+
+    own.wait()
+
+    @pl.when(me > 0)
+    def _():
+        for copy in up:
+            copy.wait_send()
+        for copy in down:
+            copy.wait_recv()
+
+    @pl.when(me < n - 1)
+    def _():
+        for copy in down:
+            copy.wait_send()
+        for copy in up:
+            copy.wait_recv()
+
+    column = lax.broadcasted_iota(jnp.int32, (levels, width), 1)
+
+    def k_row(which, r):
+        return jnp.broadcast_to(coef[which, pl.ds(r + pad - SUB, 1), :], (levels, width))
+
+    for step in range(SUB):
+        low, high = step + 1, rows + 2 * SUB - 1 - step
+
+        def body(r, carry):
+            from_above, here = carry
+            below = field[r + 1]
+            k_n, k_s, k_w, k_e = (k_row(i, r) for i in range(4))
+            g_west = pltpu.roll(k_w * here, width - 1, 1)
+            g_east = pltpu.roll(k_e * here, 1, 1)
+            g_west = jnp.where(column == width - 1, 0.0, g_west)
+            g_east = jnp.where(column == 0, 0.0, g_east)
+            new = here * (1.0 - (k_n + k_s + k_w + k_e)) + k_row(0, r + 1) * below
+            new = new + from_above + g_west + g_east
+            if step == SUB - 1:
+                for c in range(tiles):
+                    turned[c, pl.ds(r - SUB, levels, stride=rows), :] = new[:, c * 128 : (c + 1) * 128]
+            else:
+                field[r] = new
+            return (k_s * here, below)
+
+        lax.fori_loop(low, high, body, (k_row(1, low - 1) * field[low - 1], field[low]))
+
+    for c in range(tiles):
+        grad_ref[:, c * 128 : (c + 1) * 128] = turned[c]
+    for copy in copies:
+        copy.wait()
+    ids = received[levels]
+    named = jnp.where(ids == lax.broadcasted_iota(jnp.int32, ids.shape, 1).astype(jnp.float32), 1.0, 0.0)
+    place = named.T[:HOST_BLK].astype(jnp.bfloat16)
+    for l in range(levels):
+        host_ref[pl.ds(l, HOST_BLK, stride=levels), :] = split_dot(place, received[l])
+
+
+def fused(n, capacity, adjoint, coeffs, dist, sources, weights, owners, slots, counts):
+    levels, rows, width = adjoint.shape
+    nblk, block = sources.shape
+    host_width = weights.shape[2]
+    places = n * capacity
+    last = width // 128 - 1
+    whole = lambda shape: pl.BlockSpec(shape, lambda i: (0,) * len(shape))
+    packed = pl.pallas_call(
+        functools.partial(contrib_kernel, n, capacity, width),
+        grid=(nblk // STEP_BLOCKS,),
+        out_shape=jax.ShapeDtypeStruct((levels + 1, places, host_width), jnp.float32),
+        in_specs=[
+            pl.BlockSpec((STEP_BLOCKS, block), lambda i: (i, 0)),
+            pl.BlockSpec((STEP_BLOCKS, block, host_width), lambda i: (i, 0, 0)),
+            pl.BlockSpec((levels, rows, 128), lambda i: (0, 0, 0)),
+            pl.BlockSpec((levels, rows, 128), lambda i: (0, 0, last)),
+            pl.BlockSpec((rows, 128), lambda i: (0, 0)),
+            pl.BlockSpec((rows, 128), lambda i: (0, last)),
+            whole((1, nblk)),
+            whole((1, nblk)),
+            pl.BlockSpec(memory_space=pltpu.SMEM),
+        ],
+        out_specs=whole((levels + 1, places, host_width)),
+        scratch_shapes=[
+            pltpu.VMEM((rows * 2 * ZW // 128, levels, 128), jnp.float32),
+            pltpu.VMEM((levels * nblk, host_width), jnp.float32),
+        ],
+        compiler_params=pltpu.CompilerParams(vmem_limit_bytes=24 * 2**20),
+        name="contributions",
+    )(sources, weights, adjoint, adjoint, dist, dist, owners.reshape(1, nblk), slots.reshape(1, nblk), counts)
+    vmem = pl.BlockSpec(memory_space=pltpu.VMEM)
+    grad, host = pl.pallas_call(
+        functools.partial(exchange_kernel, n, capacity),
+        out_shape=[
+            jax.ShapeDtypeStruct((levels * rows, width), jnp.float32),
+            jax.ShapeDtypeStruct((HOST_BLK * levels, host_width), jnp.float32),
+        ],
+        in_specs=[vmem] * 4,
+        out_specs=[vmem, vmem],
+        scratch_shapes=[
+            pltpu.VMEM((rows + 2 * SUB, levels, width), jnp.float32),
+            pltpu.VMEM((4, rows + 16, width), jnp.float32),
+            pltpu.VMEM((width // 128, levels * rows, 128), jnp.float32),
+            pltpu.VMEM((levels + 1, places, host_width), jnp.float32),
+            pltpu.SemaphoreType.DMA((2, 2)),
+            pltpu.SemaphoreType.DMA((2, 2)),
+            pltpu.SemaphoreType.DMA,
+            pltpu.SemaphoreType.DMA((n - 1,)),
+            pltpu.SemaphoreType.DMA((n - 1,)),
+        ],
+        compiler_params=pltpu.CompilerParams(
+            collective_id=0, has_side_effects=True, vmem_limit_bytes=24 * 2**20
+        ),
+        name="exchange",
+    )(packed, adjoint.reshape(levels * rows, width), coeffs, dist)
+    return grad.reshape(levels, rows, width), host.reshape(HOST_BLK, levels, host_width)
+
+
 def local(adjoint, coeffs, dist, sources, weights, owners, slots, counts):
     levels, rows, width = adjoint.shape
     nblk = sources.shape[0]
     host_width = weights.shape[2]
     owner_count = lax.axis_size("gy")
     capacity = max(2, (2 * nblk + owner_count - 1) // owner_count)
+    if capacity % 8 == 0:
+        return fused(owner_count, capacity, adjoint, coeffs, dist, sources, weights, owners, slots, counts)
     relax = davies(dist)
     k_north, k_south, k_west, k_east = (coeffs[0], coeffs[1], coeffs[2], coeffs[3])
     total = k_north + k_south + k_west + k_east

time: 150 us -> 46.8 us (0.31)
  the two profiles are of different devices: /device:TPU:16 before, /device:TPU:11 now
where the time goes in v1:
time: 46.8 us; the launch traced here: 46.5 us
  Pallas kernels  37.5 us (80%)
  local copies, waits for them, and re-layouts  7.66 us (16%)
  between operations  1.32 us (3%)
    pallas_call x1, Pallas kernels, fused(): pl.pallas_call(functools.partial(exchange_kernel, n, capacity), out_shape...  33.9 us
    unnamed x16, local copies, waits for them, and re-layouts  7.66 us
    pallas_call x1, Pallas kernels, fused(): pl.pallas_call(functools.partial(contrib_kernel, n, capacity, width), gri...  3.55 us

profile of v1, /device:TPU:11, one launch (start us, length us, event | category | flops | bytes accessed | tf_op | source)
XLA Modules:
  0.0 46.5 jit_solution(18347481708084553427)
XLA Ops:
  1.3 0.0 copy-start
  1.3 1.0 %copy-done = f32[8,16,1024]{2,1,0:T(8,128)S(1)} copy-done((f32[8,16,1024]{2,1,0:T(8,128)S(1)}, f32[8,16,1024]{2,1,0:T(8,128)}, u32[]{:S(2)}) %copy-start) | copy-done | bytes 524312
  2.3 0.0 copy-start.1
  2.3 2.2 %copy-done.1 = bf16[128,128,128]{2,1,0:T(8,128)(2,1)S(1)} copy-done((bf16[128,128,128]{2,1,0:T(8,128)(2,1)S(1)}, bf16[128,128,128]{2,1,0:T(8,128)(2,1)}, u32[]{:S(2)}) %copy-start.1) | copy-done | bytes 4194328
  4.5 0.0 copy-start.2
  4.5 0.8 %copy-done.2 = s32[16,1024]{1,0:T(8,128)S(1)} copy-done((s32[16,1024]{1,0:T(8,128)S(1)}, s32[16,1024]{1,0:T(8,128)}, u32[]{:S(2)}) %copy-start.2) | copy-done | bytes 65560
  5.3 0.0 copy-start.4
  5.4 0.8 %copy-done.4 = s32[128,128]{1,0:T(8,128)S(1)} copy-done((s32[128,128]{1,0:T(8,128)S(1)}, s32[128,128]{1,0:T(8,128)}, u32[]{:S(2)}) %copy-start.4) | copy-done | bytes 65560
  6.2 0.0 copy-start.5
  6.2 0.7 %copy-done.5 = s32[128,1]{0,1:T(1,128)S(1)} copy-done((s32[128,1]{0,1:T(1,128)S(1)}, s32[128,1]{0,1:T(1,128)}, u32[]{:S(2)}) %copy-start.5) | copy-done | bytes 536
  6.8 0.0 copy-start.6
  6.8 0.7 %copy-done.6 = s32[128]{0:T(128)S(1)} copy-done((s32[128]{0:T(128)S(1)}, s32[128]{0:T(128)}, u32[]{:S(2)}) %copy-start.6) | copy-done | bytes 536
  7.5 0.0 copy-start.3
  7.5 3.5 %contributions.1.packed_ref = f32[9,256,128]{2,1,0:T(8,128)S(1)} custom-call(s32[128,128]{1,0:T(8,128)S(1)} %copy-done.4, bf16[128,128,128]{2,1,0:T(8,128)(2,1)S(1)} %copy-done.1, f32[8,16,1024]{2,1,0:T(8,128)S(1)} %copy-done, f32[8,16,1024]{2,1,0:T(8,128)S(1)} %copy-done, s32[16,1024]{1,0:T(8,128)S(1)} %copy-done.2, s32[16,1024]{1,0:T(8,128)S(1)} %copy-done.2, ...), custom_call_target="tpu_custom_call" | custom-call | tf_op jit(solution)/shard_map/contributions/pallas_call | solution.py:258
  11.1 0.0 copy-done.3
  11.1 33.9 %exchange.1 = (f32[128,1024]{1,0:T(8,128)S(1)}, f32[256,128]{1,0:T(8,128)S(1)}) custom-call(f32[9,256,128]{2,1,0:T(8,128)S(1)} %contributions.1.packed_ref, f32[128,1024]{1,0:T(8,128)S(1)} %bitcast.5, f32[4,16,1024]{2,1,0:T(8,128)S(1)} %copy-done.3, s32[16,1024]{1,0:T(8,128)S(1)} %copy-done.2), custom_call_target="tpu_custom_call" | custom-call | tf_op jit(solution)/shard_map/exchange/pallas_call | solution.py:282
  45.0 0.8 %copy.13 = f32[8,16,1024]{2,1,0:T(8,128)} copy(f32[8,16,1024]{2,1,0:T(8,128)S(1)} %bitcast.6) | data formatting | bytes 1048576
  45.8 0.7 %copy.14 = f32[32,8,128]{2,1,0:T(8,128)} copy(f32[32,8,128]{2,1,0:T(8,128)S(1)} %bitcast.7) | data formatting | bytes 262144
Async XLA Ops:
  1.3 1.0 %copy-start = (f32[8,16,1024]{2,1,0:T(8,128)S(1)}, f32[8,16,1024]{2,1,0:T(8,128)}, u32[]{:S(2)}) copy-start(f32[8,16,1024]{2,1,0:T(8,128)} %right_ref.1) | copy-start | bytes 1572868
  2.3 2.2 %copy-start.1 = (bf16[128,128,128]{2,1,0:T(8,128)(2,1)S(1)}, bf16[128,128,128]{2,1,0:T(8,128)(2,1)}, u32[]{:S(2)}) copy-start(bf16[128,128,128]{2,1,0:T(8,128)(2,1)} %w_ref.1) | copy-start | bytes 12582916
  4.5 0.8 %copy-start.2 = (s32[16,1024]{1,0:T(8,128)S(1)}, s32[16,1024]{1,0:T(8,128)}, u32[]{:S(2)}) copy-start(s32[16,1024]{1,0:T(8,128)} %dist_ref.1) | copy-start | bytes 196612
  5.3 0.8 %copy-start.4 = (s32[128,128]{1,0:T(8,128)S(1)}, s32[128,128]{1,0:T(8,128)}, u32[]{:S(2)}) copy-start(s32[128,128]{1,0:T(8,128)} %src_ref.1) | copy-start | bytes 196612
  6.2 0.7 %copy-start.5 = (s32[128,1]{0,1:T(1,128)S(1)}, s32[128,1]{0,1:T(1,128)}, u32[]{:S(2)}) copy-start(s32[128,1]{0,1:T(1,128)} %param.13) | copy-start | bytes 1540
  6.8 0.7 %copy-start.6 = (s32[128]{0:T(128)S(1)}, s32[128]{0:T(128)}, u32[]{:S(2)}) copy-start(s32[128]{0:T(128)} %param.14) | copy-start | bytes 1540
  7.5 3.6 %copy-start.3 = (f32[4,16,1024]{2,1,0:T(8,128)S(1)}, f32[4,16,1024]{2,1,0:T(8,128)}, u32[]{:S(2)}) copy-start(f32[4,16,1024]{2,1,0:T(8,128)} %coeffs_ref.1) | copy-start | bytes 786436

commit v2 on v0

--- a/solution.py
+++ b/solution.py
@@ -1,11 +1,19 @@
+import functools
+
 import jax
 import jax.numpy as jnp
 from jax import lax
+from jax.experimental import pallas as pl
+from jax.experimental.pallas import tpu as pltpu
 from jax.sharding import PartitionSpec as P
 
 ZW = 16
 SUB = 4
 HOST_BLK = 32
+STEP_BLOCKS = 16
+W_PARTS = 4
+CHUNK = 2
+MESH = pl.DeviceIdType.MESH
 
 
 def from_behind(value, axis, steps):
@@ -28,12 +36,351 @@
     return (left_part, right_part)
 
 
+def split_dot(onehot, x):
+    hi = x.astype(jnp.bfloat16)
+    lo = (x - hi.astype(jnp.float32)).astype(jnp.bfloat16)
+    return jnp.dot(onehot, hi, preferred_element_type=jnp.float32) + jnp.dot(
+        onehot, lo, preferred_element_type=jnp.float32
+    )
+
+
+def fused_kernel(
+    n, sizes, adjoint_hbm, coeffs_hbm, dist_hbm, sources_hbm, weights_hbm, owner_ref, slot_ref, count_ref,
+    grad_ref, host_ref,
+    adjoint_ref, dist_ref, src_ref, w_ref, table, contrib, field, coef, stage, got_stage, turned,
+    dense, got_core, half, got_x, quarter, got_z,
+    in_sem, w_sem, halo_send, halo_recv, core_send, core_recv, x_send, x_recv, z_send, z_recv,
+):
+    nz, nx, nc = sizes
+    me = lax.axis_index("gy")
+    my_z, my_x, my_c = me // (nx * nc), (me // nc) % nx, me % nc
+    rows, width = dist_ref.shape
+    levels = adjoint_ref.shape[0] // rows
+    nblk, lanes = src_ref.shape
+    tiles = width // lanes
+    pad = 8
+    per = lanes // (2 * ZW)
+
+    def at_gy(z, x, c):
+        return {"gy": (z * nx + x) * nc + c}
+
+    core_peer = at_gy(my_z, my_x, 1 - my_c)
+    x_peer = at_gy(my_z, 1 - my_x, my_c)
+    z_peers = [at_gy(lax.rem(my_z + k, nz), my_x, my_c) for k in range(1, nz)]
+
+    barrier = pltpu.get_barrier_semaphore()
+    around = [{"gy": lax.rem(me + n - 1, n)}, {"gy": lax.rem(me + 1, n)}]
+    partners = [core_peer, x_peer] + z_peers + around
+    for peer in partners:
+        pl.semaphore_signal(barrier, inc=1, device_id=peer, device_id_type=MESH)
+
+    loads = [
+        pltpu.make_async_copy(source, target, in_sem.at[i])
+        for i, (source, target) in enumerate(
+            [
+                (dist_hbm, dist_ref),
+                (adjoint_hbm, adjoint_ref),
+                (coeffs_hbm, coef.at[:, pad : pad + rows, :]),
+                (sources_hbm, src_ref),
+            ]
+        )
+    ]
+    for load in loads:
+        load.start()
+    w_loads = []
+    for i in range(W_PARTS):
+        part = pl.ds(i * (nblk // W_PARTS), nblk // W_PARTS)
+        w_loads.append(pltpu.make_async_copy(weights_hbm.at[part], w_ref.at[part], w_sem.at[i]))
+        w_loads[-1].start()
+
+    for load in loads:
+        load.wait()
+    for c in range(tiles):
+        turned[c] = adjoint_ref[:, c * lanes : (c + 1) * lanes]
+
+    @pl.loop(0, rows)
+    def _(r):
+        keep = 1.0 - davies(dist_ref[pl.ds(r, 1), :])
+        for c in range(tiles):
+            cut = slice(c * lanes, (c + 1) * lanes)
+            field[r + SUB, :, cut] = keep[:, cut] * turned[c, pl.ds(r, levels, stride=rows), :]
+
+    for i in range(4):
+        spot = slice(i % 2 * SUB, (i % 2 + 1) * SUB)
+        stage[0, i // 2, spot] = coef[i, pad : pad + SUB, :]
+        stage[1, i // 2, spot] = coef[i, pad + rows - SUB : pad + rows, :]
+
+    pl.semaphore_wait(barrier, len(partners))
+
+    def halo(at):
+        to = {"gy": me - 1 if at == 0 else me + 1}
+        first = SUB if at == 0 else rows
+        land = rows + SUB if at == 0 else 0
+        return [
+            pltpu.make_async_remote_copy(
+                src_ref=field.at[first : first + SUB],
+                dst_ref=field.at[land : land + SUB],
+                send_sem=halo_send.at[at, 0],
+                recv_sem=halo_recv.at[at, 0],
+                device_id=to,
+                device_id_type=MESH,
+            ),
+            pltpu.make_async_remote_copy(
+                src_ref=stage.at[at],
+                dst_ref=got_stage.at[at],
+                send_sem=halo_send.at[at, 1],
+                recv_sem=halo_recv.at[at, 1],
+                device_id=to,
+                device_id_type=MESH,
+            ),
+        ]
+
+    up, down = halo(0), halo(1)
+
+    @pl.when(me > 0)
+    def _():
+        for copy in up:
+            copy.start()
+
+    @pl.when(me < n - 1)
+    def _():
+        for copy in down:
+            copy.start()
+
+    lane = lax.broadcasted_iota(jnp.int32, (levels, lanes), 1)
+    for q in range(rows // per):
+        tile = jnp.zeros((levels, lanes), jnp.float32)
+        for i in range(per):
+            r = q * per + i
+            z_left = davies(dist_ref[r : r + 1, :lanes]) * turned[0, pl.ds(r, levels, stride=rows), :]
+            z_right = davies(dist_ref[r : r + 1, width - lanes :]) * turned[tiles - 1, pl.ds(r, levels, stride=rows), :]
+            both = jnp.where(lane < lanes // 2, z_left, z_right)
+            both = pltpu.roll(both, (ZW + 2 * ZW * i) % lanes, 1)
+            tile = jnp.where((lane >= 2 * ZW * i) & (lane < 2 * ZW * (i + 1)), both, tile)
+        table[q] = tile
+
+    for part in range(W_PARTS):
+        w_loads[part].wait()
+
+        @pl.loop(part * (nblk // W_PARTS // STEP_BLOCKS), (part + 1) * (nblk // W_PARTS // STEP_BLOCKS))
+        def _(step):
+            base = pl.multiple_of(step * STEP_BLOCKS, STEP_BLOCKS)
+            src = src_ref[pl.ds(base, STEP_BLOCKS), :]
+            row = src // width
+            col = src - row * width
+            spot = jnp.where(col < ZW, col + ZW, col - (width - ZW)) + (row % per) * (2 * ZW)
+            group = row // per
+            for j in range(STEP_BLOCKS):
+                at = jnp.broadcast_to(spot[j : j + 1, :], (levels, lanes))
+                which = jnp.broadcast_to(group[j : j + 1, :], (levels, lanes))
+                value = jnp.take_along_axis(table[0], at, axis=1)
+                for q in range(1, rows // per):
+                    value = jnp.where(which == q, jnp.take_along_axis(table[q], at, axis=1), value)
+                out = jnp.dot(value.astype(jnp.bfloat16), w_ref[base + j], preferred_element_type=jnp.float32)
+                contrib[pl.ds(base + j, levels, stride=nblk), :] = out
+
+    owner = owner_ref[...]
+    own_z, own_x, own_c = owner // (nx * nc), (owner // nc) % nx, owner % nc
+    target = ((own_c * nx + own_x) * nz + own_z) * HOST_BLK + slot_ref[...]
+    live = lax.broadcasted_iota(jnp.int32, (1, nblk), 1) < count_ref[0]
+    target = jnp.where(live, target, -1)
+    hosts = n * HOST_BLK
+    hit = lax.broadcasted_iota(jnp.int32, (hosts, nblk), 0) == target
+    place = jnp.where(hit, 1.0, 0.0).astype(jnp.bfloat16)
+
+    count = levels // CHUNK
+    part_of = lambda i: pl.ds(i * CHUNK, CHUNK)
+    sent = []
+    for i in range(count):
+        for l in range(i * CHUNK, (i + 1) * CHUNK):
+            full = split_dot(place, contrib[l * nblk : (l + 1) * nblk, :])
+            dense[l] = full.reshape(nc, nx, nz, HOST_BLK, lanes)
+        sent.append(
+            pltpu.make_async_remote_copy(
+                src_ref=dense.at[part_of(i), 1 - my_c],
+                dst_ref=got_core.at[part_of(i)],
+                send_sem=core_send.at[i],
+                recv_sem=core_recv.at[i],
+                device_id=core_peer,
+                device_id_type=MESH,
+            )
+        )
+        sent[-1].start()
+    for i in range(count):
+        sent[i].wait()
+        half[part_of(i)] = dense[part_of(i), my_c] + got_core[part_of(i)]
+        sent.append(
+            pltpu.make_async_remote_copy(
+                src_ref=half.at[part_of(i), 1 - my_x],
+                dst_ref=got_x.at[part_of(i)],
+                send_sem=x_send.at[i],
+                recv_sem=x_recv.at[i],
+                device_id=x_peer,
+                device_id_type=MESH,
+            )
+        )
+        sent[-1].start()
+
+    @pl.when(me == 0)
+    def _():
+        field[0:SUB] = jnp.zeros((SUB, levels, width), jnp.float32)
+        got_stage[1] = jnp.zeros(got_stage.shape[1:], jnp.float32)
+
+    @pl.when(me == n - 1)
+    def _():
+        field[rows + SUB :] = jnp.zeros((SUB, levels, width), jnp.float32)
+        got_stage[0] = jnp.zeros(got_stage.shape[1:], jnp.float32)
+
+    @pl.when(me > 0)
+    def _():
+        for copy in up:
+            copy.wait_send()
+        for copy in down:
+            copy.wait_recv()
+
+    @pl.when(me < n - 1)
+    def _():
+        for copy in down:
+            copy.wait_send()
+        for copy in up:
+            copy.wait_recv()
+
+    for i in range(4):
+        spot = slice(i % 2 * SUB, (i % 2 + 1) * SUB)
+        coef[i, pad - SUB : pad, :] = got_stage[1, i // 2, spot]
+        coef[i, pad + rows : pad + rows + SUB, :] = got_stage[0, i // 2, spot]
+
+    column = lax.broadcasted_iota(jnp.int32, (levels, width), 1)
+
+    def k_row(which, r):
+        return jnp.broadcast_to(coef[which, pl.ds(r + pad - SUB, 1), :], (levels, width))
+
+    def sweep(step):
+        low, high = step + 1, rows + 2 * SUB - 1 - step
+
+        def body(r, carry):
+            from_above, here = carry
+            below = field[r + 1]
+            k_n, k_s, k_w, k_e = (k_row(i, r) for i in range(4))
+            g_west = pltpu.roll(k_w * here, width - 1, 1)
+            g_east = pltpu.roll(k_e * here, 1, 1)
+            g_west = jnp.where(column == width - 1, 0.0, g_west)
+            g_east = jnp.where(column == 0, 0.0, g_east)
+            new = here * (1.0 - (k_n + k_s + k_w + k_e)) + k_row(0, r + 1) * below
+            new = new + from_above + g_west + g_east
+            if step == SUB - 1:
+                for c in range(tiles):
+                    turned[c, pl.ds(r - SUB, levels, stride=rows), :] = new[:, c * lanes : (c + 1) * lanes]
+            else:
+                field[r] = new
+            return (k_s * here, below)
+
+        lax.fori_loop(low, high, body, (k_row(1, low - 1) * field[low - 1], field[low]))
+
+    z_sent = []
+
+    def along_z(i):
+        sent[count + i].wait()
+        quarter[part_of(i)] = half[part_of(i), my_x] + got_x[part_of(i)]
+        for k in range(1, nz):
+            z_sent.append(
+                pltpu.make_async_remote_copy(
+                    src_ref=quarter.at[part_of(i), lax.rem(my_z + k, nz)],
+                    dst_ref=got_z.at[k - 1, part_of(i)],
+                    send_sem=z_send.at[i, k - 1],
+                    recv_sem=z_recv.at[i, k - 1],
+                    device_id=z_peers[k - 1],
+                    device_id_type=MESH,
+                )
+            )
+            z_sent[-1].start()
+
+    done = 0
+    for step in range(SUB):
+        sweep(step)
+        upto = count - 1 if step == SUB - 1 else (step + 1) * (count - 1) // SUB
+        for i in range(done, upto):
+            along_z(i)
+        done = upto
+    for c in range(tiles):
+        grad_ref[:, c * lanes : (c + 1) * lanes] = turned[c]
+    along_z(count - 1)
+    for i in range(count):
+        for copy in z_sent[i * (nz - 1) : (i + 1) * (nz - 1)]:
+            copy.wait()
+        for l in range(i * CHUNK, (i + 1) * CHUNK):
+            total = quarter[l, my_z]
+            for k in range(nz - 1):
+                total = total + got_z[k, l]
+            host_ref[pl.ds(l, HOST_BLK, stride=levels), :] = total
+
+
+def fused(n, sizes, adjoint, coeffs, dist, sources, weights, owners, slots, counts):
+    levels, rows, width = adjoint.shape
+    nblk, block = sources.shape
+    lanes = weights.shape[2]
+    nz, nx, nc = sizes
+    count = levels // CHUNK
+    f32 = lambda *shape: pltpu.VMEM(shape, jnp.float32)
+    dma = lambda *shape: pltpu.SemaphoreType.DMA(shape)
+    hbm = pl.BlockSpec(memory_space=pltpu.HBM)
+    vmem = pl.BlockSpec(memory_space=pltpu.VMEM)
+    grad, host = pl.pallas_call(
+        functools.partial(fused_kernel, n, sizes),
+        out_shape=[
+            jax.ShapeDtypeStruct((levels * rows, width), jnp.float32),
+            jax.ShapeDtypeStruct((HOST_BLK * levels, lanes), jnp.float32),
+        ],
+        in_specs=[hbm] * 5 + [vmem] * 2 + [pl.BlockSpec(memory_space=pltpu.SMEM)],
+        out_specs=[vmem, vmem],
+        scratch_shapes=[
+            f32(levels * rows, width),
+            pltpu.VMEM((rows, width), jnp.int32),
+            pltpu.VMEM((nblk, block), jnp.int32),
+            pltpu.VMEM((nblk, block, lanes), jnp.bfloat16),
+            f32(rows * 2 * ZW // lanes, levels, lanes),
+            f32(levels * nblk, lanes),
+            f32(rows + 2 * SUB, levels, width),
+            f32(4, rows + 16, width),
+            f32(2, 2, 2 * SUB, width),
+            f32(2, 2, 2 * SUB, width),
+            f32(width // lanes, levels * rows, lanes),
+            f32(levels, nc, nx, nz, HOST_BLK, lanes),
+            f32(levels, nx, nz, HOST_BLK, lanes),
+            f32(levels, nx, nz, HOST_BLK, lanes),
+            f32(levels, nz, HOST_BLK, lanes),
+            f32(levels, nz, HOST_BLK, lanes),
+            f32(nz - 1, levels, HOST_BLK, lanes),
+            dma(4),
+            dma(W_PARTS),
+            dma(2, 2),
+            dma(2, 2),
+            dma(count),
+            dma(count),
+            dma(count),
+            dma(count),
+            dma(count, nz - 1),
+            dma(count, nz - 1),
+        ],
+        compiler_params=pltpu.CompilerParams(
+            collective_id=0, has_side_effects=True, vmem_limit_bytes=62 * 2**20
+        ),
+        name="fused",
+    )(
+        adjoint.reshape(levels * rows, width), coeffs, dist, sources, weights,
+        owners.reshape(1, nblk), slots.reshape(1, nblk), counts,
+    )
+    return grad.reshape(levels, rows, width), host.reshape(HOST_BLK, levels, lanes)
+
+
 def local(adjoint, coeffs, dist, sources, weights, owners, slots, counts):
     levels, rows, width = adjoint.shape
     nblk = sources.shape[0]
     host_width = weights.shape[2]
     owner_count = lax.axis_size("gy")
     capacity = max(2, (2 * nblk + owner_count - 1) // owner_count)
+    if owner_count == 16:
+        return fused(owner_count, (4, 2, 2), adjoint, coeffs, dist, sources, weights, owners, slots, counts)
     relax = davies(dist)
     k_north, k_south, k_west, k_east = (coeffs[0], coeffs[1], coeffs[2], coeffs[3])
     total = k_north + k_south + k_west + k_east

time: 150 us -> 35.4 us (0.24)
  the two profiles are of different devices: /device:TPU:16 before, /device:TPU:0 now
where the time goes in v2:
time: 35.4 us; the launch traced here: 35.2 us
  Pallas kernels  30.4 us (86%)
  local copies, waits for them, and re-layouts  3.45 us (10%)
  between operations  1.29 us (4%)
    pallas_call x1, Pallas kernels, fused(): pl.pallas_call(functools.partial(fused_kernel, n, sizes), out_shape=[jax....  30.4 us
    unnamed x2, local copies, waits for them, and re-layouts  3.45 us

profile of v2, /device:TPU:0, one launch (start us, length us, event | category | flops | bytes accessed | tf_op | source)
XLA Modules:
  0.0 35.2 jit_solution(18338590253474603296)
XLA Ops:
  1.3 30.4 %fused.1 = (f32[128,1024]{1,0:T(8,128)}, f32[256,128]{1,0:T(8,128)}) custom-call(f32[128,1024]{1,0:T(8,128)} %bitcast.5, f32[4,16,1024]{2,1,0:T(8,128)} %coeffs_hbm.1, s32[16,1024]{1,0:T(8,128)} %dist_hbm.1, s32[128,128]{1,0:T(8,128)} %sources_hbm.1, bf16[128,128,128]{2,1,0:T(8,128)(2,1)} %weights_hbm.1, s32[1,128]{1,0:T(1,128)} %bitcast.8, ...), custom_call_target="tpu_custom_call" | custom-call | tf_op jit(solution)/shard_map/fused/pallas_call | solution.py:328
  31.7 1.9 %copy.13 = f32[8,16,1024]{2,1,0:T(8,128)} copy(f32[8,16,1024]{2,1,0:T(8,128)} %bitcast.6) | data formatting | bytes 1048576
  33.6 1.6 %copy.14 = f32[32,8,128]{2,1,0:T(8,128)} copy(f32[32,8,128]{2,1,0:T(8,128)} %bitcast.7) | data formatting | bytes 262144

commit v3 on v2

--- a/solution.py
+++ b/solution.py
@@ -12,7 +12,7 @@
 HOST_BLK = 32
 STEP_BLOCKS = 16
 W_PARTS = 4
-CHUNK = 2
+Z_AFTER = (3, 6, 8)
 MESH = pl.DeviceIdType.MESH
 
 
@@ -44,12 +44,28 @@
     )
 
 
+def chunks_of(levels):
+    sizes = [2] * (levels // 2 - 1) + [1, 1]
+    return [(sum(sizes[:i]), size) for i, size in enumerate(sizes)]
+
+
+def deliver_kernel(grad_in, host_in, grad_ref, host_ref, sem):
+    copies = [
+        pltpu.make_async_copy(grad_in, grad_ref, sem.at[0]),
+        pltpu.make_async_copy(host_in, host_ref, sem.at[1]),
+    ]
+    for copy in copies:
+        copy.start()
+    for copy in copies:
+        copy.wait()
+
+
 def fused_kernel(
     n, sizes, adjoint_hbm, coeffs_hbm, dist_hbm, sources_hbm, weights_hbm, owner_ref, slot_ref, count_ref,
     grad_ref, host_ref,
     adjoint_ref, dist_ref, src_ref, w_ref, table, contrib, field, coef, stage, got_stage, turned,
     dense, got_core, half, got_x, quarter, got_z,
-    in_sem, w_sem, halo_send, halo_recv, core_send, core_recv, x_send, x_recv, z_send, z_recv,
+    in_sem, w_sem, out_sem, halo_send, halo_recv, core_send, core_recv, x_send, x_recv, z_send, z_recv,
 ):
     nz, nx, nc = sizes
     me = lax.axis_index("gy")
@@ -188,14 +204,16 @@
     hit = lax.broadcasted_iota(jnp.int32, (hosts, nblk), 0) == target
     place = jnp.where(hit, 1.0, 0.0).astype(jnp.bfloat16)
 
-    count = levels // CHUNK
-    part_of = lambda i: pl.ds(i * CHUNK, CHUNK)
-    sent = []
-    for i in range(count):
-        for l in range(i * CHUNK, (i + 1) * CHUNK):
+    cuts = chunks_of(levels)
+    count = len(cuts)
+    part_of = lambda i: pl.ds(*cuts[i])
+    core_sent, x_sent, z_sent = [], [], []
+
+    def to_core(i):
+        for l in range(cuts[i][0], sum(cuts[i])):
             full = split_dot(place, contrib[l * nblk : (l + 1) * nblk, :])
             dense[l] = full.reshape(nc, nx, nz, HOST_BLK, lanes)
-        sent.append(
+        core_sent.append(
             pltpu.make_async_remote_copy(
                 src_ref=dense.at[part_of(i), 1 - my_c],
                 dst_ref=got_core.at[part_of(i)],
@@ -205,11 +223,12 @@
                 device_id_type=MESH,
             )
         )
-        sent[-1].start()
-    for i in range(count):
-        sent[i].wait()
-        half[part_of(i)] = dense[part_of(i), my_c] + got_core[part_of(i)]
-        sent.append(
+        core_sent[i].start()
+
+    def along_x(i):
+        core_sent[i].wait()
+        half[part_of(i), 1 - my_x] = dense[part_of(i), my_c, 1 - my_x] + got_core[part_of(i), 1 - my_x]
+        x_sent.append(
             pltpu.make_async_remote_copy(
                 src_ref=half.at[part_of(i), 1 - my_x],
                 dst_ref=got_x.at[part_of(i)],
@@ -219,7 +238,14 @@
                 device_id_type=MESH,
             )
         )
-        sent[-1].start()
+        x_sent[i].start()
+        half[part_of(i), my_x] = dense[part_of(i), my_c, my_x] + got_core[part_of(i), my_x]
+
+    for i in range(count):
+        to_core(i)
+        if i > 0:
+            along_x(i - 1)
+    along_x(count - 1)
 
     @pl.when(me == 0)
     def _():
@@ -255,8 +281,7 @@
     def k_row(which, r):
         return jnp.broadcast_to(coef[which, pl.ds(r + pad - SUB, 1), :], (levels, width))
 
-    def sweep(step):
-        low, high = step + 1, rows + 2 * SUB - 1 - step
+    def sweep(step, low, high, carry):
 
         def body(r, carry):
             from_above, here = carry
@@ -275,12 +300,12 @@
                 field[r] = new
             return (k_s * here, below)
 
-        lax.fori_loop(low, high, body, (k_row(1, low - 1) * field[low - 1], field[low]))
-
-    z_sent = []
+        if carry is None:
+            carry = (k_row(1, low - 1) * field[low - 1], field[low])
+        return lax.fori_loop(low, high, body, carry)
 
     def along_z(i):
-        sent[count + i].wait()
+        x_sent[i].wait()
         quarter[part_of(i)] = half[part_of(i), my_x] + got_x[part_of(i)]
         for k in range(1, nz):
             z_sent.append(
@@ -297,22 +322,33 @@
 
     done = 0
     for step in range(SUB):
-        sweep(step)
-        upto = count - 1 if step == SUB - 1 else (step + 1) * (count - 1) // SUB
-        for i in range(done, upto):
-            along_z(i)
-        done = upto
-    for c in range(tiles):
-        grad_ref[:, c * lanes : (c + 1) * lanes] = turned[c]
-    along_z(count - 1)
+        low, high = step + 1, rows + 2 * SUB - 1 - step
+        carry = sweep(step, low, (low + high) // 2, None)
+        if 2 * step + 1 in Z_AFTER:
+            along_z(done)
+            done += 1
+        sweep(step, (low + high) // 2, high, carry)
+        if 2 * step + 2 in Z_AFTER:
+            along_z(done)
+            done += 1
+    grads = [
+        pltpu.make_async_copy(turned.at[c], grad_ref.at[:, c * lanes : (c + 1) * lanes], out_sem.at[c])
+        for c in range(tiles)
+    ]
+    for copy in grads:
+        copy.start()
+    for i in range(done, count):
+        along_z(i)
     for i in range(count):
         for copy in z_sent[i * (nz - 1) : (i + 1) * (nz - 1)]:
             copy.wait()
-        for l in range(i * CHUNK, (i + 1) * CHUNK):
+        for l in range(cuts[i][0], sum(cuts[i])):
             total = quarter[l, my_z]
             for k in range(nz - 1):
                 total = total + got_z[k, l]
             host_ref[pl.ds(l, HOST_BLK, stride=levels), :] = total
+    for copy in grads:
+        copy.wait()
 
 
 def fused(n, sizes, adjoint, coeffs, dist, sources, weights, owners, slots, counts):
@@ -320,7 +356,7 @@
     nblk, block = sources.shape
     lanes = weights.shape[2]
     nz, nx, nc = sizes
-    count = levels // CHUNK
+    count = len(chunks_of(levels))
     f32 = lambda *shape: pltpu.VMEM(shape, jnp.float32)
     dma = lambda *shape: pltpu.SemaphoreType.DMA(shape)
     hbm = pl.BlockSpec(memory_space=pltpu.HBM)
@@ -332,7 +368,7 @@
             jax.ShapeDtypeStruct((HOST_BLK * levels, lanes), jnp.float32),
         ],
         in_specs=[hbm] * 5 + [vmem] * 2 + [pl.BlockSpec(memory_space=pltpu.SMEM)],
-        out_specs=[vmem, vmem],
+        out_specs=[hbm, vmem],
         scratch_shapes=[
             f32(levels * rows, width),
             pltpu.VMEM((rows, width), jnp.int32),
@@ -353,6 +389,7 @@
             f32(nz - 1, levels, HOST_BLK, lanes),
             dma(4),
             dma(W_PARTS),
+            dma(width // lanes),
             dma(2, 2),
             dma(2, 2),
             dma(count),
@@ -370,7 +407,20 @@
         adjoint.reshape(levels * rows, width), coeffs, dist, sources, weights,
         owners.reshape(1, nblk), slots.reshape(1, nblk), counts,
     )
-    return grad.reshape(levels, rows, width), host.reshape(HOST_BLK, levels, lanes)
+    grad = grad.reshape(levels, rows, width)
+    host = host.reshape(HOST_BLK, levels, lanes)
+    return pl.pallas_call(
+        deliver_kernel,
+        out_shape=[
+            jax.ShapeDtypeStruct(grad.shape, jnp.float32),
+            jax.ShapeDtypeStruct(host.shape, jnp.float32),
+        ],
+        in_specs=[hbm, hbm],
+        out_specs=[hbm, hbm],
+        scratch_shapes=[dma(2)],
+        compiler_params=pltpu.CompilerParams(vmem_limit_bytes=62 * 2**20),
+        name="deliver",
+    )(grad, host)
 
 
 def local(adjoint, coeffs, dist, sources, weights, owners, slots, counts):

time: 35.4 us -> 53.5 us (1.51)
  Pallas kernels: 30.4 us -> 52.1 us
  local copies, waits for them, and re-layouts: 3.45 us -> 0 us
    pallas_call x0 -> x1, Pallas kernels: none -> 21 us  [fused(): pl.pallas_call(deliver_kernel, out_shape=[jax.ShapeDtypeStruct(grad.shape...]
    unnamed x2 -> x0, local copies, waits for them, and re-layouts: 3.45 us -> none
    pallas_call x1, Pallas kernels: 30.4 us -> 31.1 us  [fused(): pl.pallas_call(functools.partial(fused_kernel, n, sizes), out_shape=[jax....]
where the time goes in v3:
time: 53.5 us; the launch traced here: 53.3 us
  Pallas kernels  52.1 us (97%)
  between operations  1.29 us (2%)
    pallas_call x1, Pallas kernels, fused(): pl.pallas_call(functools.partial(fused_kernel, n, sizes), out_shape=[jax....  31.1 us
    pallas_call x1, Pallas kernels, fused(): pl.pallas_call(deliver_kernel, out_shape=[jax.ShapeDtypeStruct(grad.shape...  21 us

profile of v3, /device:TPU:0, one launch (start us, length us, event | category | flops | bytes accessed | tf_op | source)
XLA Modules:
  0.0 53.3 jit_solution(8331928916862459952)
XLA Ops:
  1.3 31.1 %fused.1 = (f32[128,1024]{1,0:T(8,128)}, f32[256,128]{1,0:T(8,128)}) custom-call(f32[128,1024]{1,0:T(8,128)} %bitcast.5, f32[4,16,1024]{2,1,0:T(8,128)} %coeffs_hbm.1, s32[16,1024]{1,0:T(8,128)} %dist_hbm.1, s32[128,128]{1,0:T(8,128)} %sources_hbm.1, bf16[128,128,128]{2,1,0:T(8,128)(2,1)} %weights_hbm.1, s32[1,128]{1,0:T(1,128)} %bitcast.8, ...), custom_call_target="tpu_custom_call" | custom-call | tf_op jit(solution)/shard_map/fused/pallas_call | solution.py:364
  32.4 21.0 %deliver.1 = (f32[8,16,1024]{2,1,0:T(8,128)}, f32[32,8,128]{2,1,0:T(8,128)}) custom-call(f32[8,16,1024]{2,1,0:T(8,128)} %bitcast.6, f32[32,8,128]{2,1,0:T(8,128)} %bitcast.7), custom_call_target="tpu_custom_call" | custom-call | tf_op jit(solution)/shard_map/deliver/pallas_call | solution.py:412

commit v4 on v3

--- a/solution.py
+++ b/solution.py
@@ -49,14 +49,19 @@
     return [(sum(sizes[:i]), size) for i, size in enumerate(sizes)]
 
 
-def deliver_kernel(grad_in, host_in, grad_ref, host_ref, sem):
-    copies = [
-        pltpu.make_async_copy(grad_in, grad_ref, sem.at[0]),
-        pltpu.make_async_copy(host_in, host_ref, sem.at[1]),
-    ]
-    for copy in copies:
+def deliver_kernel(grad_in, host_in, grad_ref, host_ref, grad_held, host_held, in_sem, out_sem):
+    levels = grad_in.shape[0]
+    parts = levels // 2
+    trips = [(grad_in.at[pl.ds(2 * i, 2)], grad_held.at[pl.ds(2 * i, 2)], grad_ref.at[pl.ds(2 * i, 2)]) for i in range(parts)]
+    trips.append((host_in, host_held, host_ref))
+    arriving = [pltpu.make_async_copy(a, b, in_sem.at[i]) for i, (a, b, c) in enumerate(trips)]
+    leaving = [pltpu.make_async_copy(b, c, out_sem.at[i]) for i, (a, b, c) in enumerate(trips)]
+    for copy in arriving:
         copy.start()
-    for copy in copies:
+    for i in range(len(trips)):
+        arriving[i].wait()
+        leaving[i].start()
+    for copy in leaving:
         copy.wait()
 
 
@@ -417,7 +422,7 @@
         ],
         in_specs=[hbm, hbm],
         out_specs=[hbm, hbm],
-        scratch_shapes=[dma(2)],
+        scratch_shapes=[f32(*grad.shape), f32(*host.shape), dma(levels // 2 + 1), dma(levels // 2 + 1)],
         compiler_params=pltpu.CompilerParams(vmem_limit_bytes=62 * 2**20),
         name="deliver",
     )(grad, host)

time: 53.5 us -> 34.4 us (0.64)
  Pallas kernels: 52.1 us -> 33 us
    pallas_call x1, Pallas kernels: 21 us -> 1.91 us  [fused(): pl.pallas_call(deliver_kernel, out_shape=[jax.ShapeDtypeStruct(grad.shape...]
where the time goes in v4:
time: 34.4 us; the launch traced here: 34.3 us
  Pallas kernels  33 us (96%)
  between operations  1.29 us (4%)
    pallas_call x1, Pallas kernels, fused(): pl.pallas_call(functools.partial(fused_kernel, n, sizes), out_shape=[jax....  31.1 us
    pallas_call x1, Pallas kernels, fused(): pl.pallas_call(deliver_kernel, out_shape=[jax.ShapeDtypeStruct(grad.shape...  1.91 us

profile of v4, /device:TPU:0, one launch (start us, length us, event | category | flops | bytes accessed | tf_op | source)
XLA Modules:
  0.0 34.3 jit_solution(17408187237339006560)
XLA Ops:
  1.3 31.1 %fused.1 = (f32[128,1024]{1,0:T(8,128)}, f32[256,128]{1,0:T(8,128)}) custom-call(f32[128,1024]{1,0:T(8,128)} %bitcast.5, f32[4,16,1024]{2,1,0:T(8,128)} %coeffs_hbm.1, s32[16,1024]{1,0:T(8,128)} %dist_hbm.1, s32[128,128]{1,0:T(8,128)} %sources_hbm.1, bf16[128,128,128]{2,1,0:T(8,128)(2,1)} %weights_hbm.1, s32[1,128]{1,0:T(1,128)} %bitcast.8, ...), custom_call_target="tpu_custom_call" | custom-call | tf_op jit(solution)/shard_map/fused/pallas_call | solution.py:369
  32.4 1.9 %deliver.1 = (f32[8,16,1024]{2,1,0:T(8,128)}, f32[32,8,128]{2,1,0:T(8,128)}) custom-call(f32[8,16,1024]{2,1,0:T(8,128)} %bitcast.6, f32[32,8,128]{2,1,0:T(8,128)} %bitcast.7), custom_call_target="tpu_custom_call" | custom-call | tf_op jit(solution)/shard_map/deliver/pallas_call | solution.py:417

commit v5 on v4

--- a/solution.py
+++ b/solution.py
@@ -12,7 +12,7 @@
 HOST_BLK = 32
 STEP_BLOCKS = 16
 W_PARTS = 4
-Z_AFTER = (3, 6, 8)
+Z_AFTER = (3, 5, 7, 8)
 MESH = pl.DeviceIdType.MESH
 
 
@@ -45,8 +45,7 @@
 
 
 def chunks_of(levels):
-    sizes = [2] * (levels // 2 - 1) + [1, 1]
-    return [(sum(sizes[:i]), size) for i, size in enumerate(sizes)]
+    return [(level, 1) for level in range(levels)]
 
 
 def deliver_kernel(grad_in, host_in, grad_ref, host_ref, grad_held, host_held, in_sem, out_sem):

time: 34.4 us -> 36.6 us (1.064)
  Pallas kernels: 33 us -> 35.2 us
    pallas_call x1, Pallas kernels: 31.1 us -> 33.3 us  [fused(): pl.pallas_call(functools.partial(fused_kernel, n, sizes), out_shape=[jax....]
where the time goes in v5:
time: 36.6 us; the launch traced here: 36.5 us
  Pallas kernels  35.2 us (96%)
  between operations  1.29 us (4%)
    pallas_call x1, Pallas kernels, fused(): pl.pallas_call(functools.partial(fused_kernel, n, sizes), out_shape=[jax....  33.3 us
    pallas_call x1, Pallas kernels, fused(): pl.pallas_call(deliver_kernel, out_shape=[jax.ShapeDtypeStruct(grad.shape...  1.91 us

profile of v5, /device:TPU:0, one launch (start us, length us, event | category | flops | bytes accessed | tf_op | source)
XLA Modules:
  0.0 36.5 jit_solution(16093211355035441625)
XLA Ops:
  1.3 33.3 %fused.1 = (f32[128,1024]{1,0:T(8,128)}, f32[256,128]{1,0:T(8,128)}) custom-call(f32[128,1024]{1,0:T(8,128)} %bitcast.5, f32[4,16,1024]{2,1,0:T(8,128)} %coeffs_hbm.1, s32[16,1024]{1,0:T(8,128)} %dist_hbm.1, s32[128,128]{1,0:T(8,128)} %sources_hbm.1, bf16[128,128,128]{2,1,0:T(8,128)(2,1)} %weights_hbm.1, s32[1,128]{1,0:T(1,128)} %bitcast.8, ...), custom_call_target="tpu_custom_call" | custom-call | tf_op jit(solution)/shard_map/fused/pallas_call | solution.py:368
  34.6 1.9 %deliver.1 = (f32[8,16,1024]{2,1,0:T(8,128)}, f32[32,8,128]{2,1,0:T(8,128)}) custom-call(f32[8,16,1024]{2,1,0:T(8,128)} %bitcast.6, f32[32,8,128]{2,1,0:T(8,128)} %bitcast.7), custom_call_target="tpu_custom_call" | custom-call | tf_op jit(solution)/shard_map/deliver/pallas_call | solution.py:416

commit v6 on v4

--- a/solution.py
+++ b/solution.py
@@ -12,7 +12,7 @@
 HOST_BLK = 32
 STEP_BLOCKS = 16
 W_PARTS = 4
-Z_AFTER = (3, 6, 8)
+Z_AFTER = (3, 5, 7)
 MESH = pl.DeviceIdType.MESH
 
 
@@ -45,7 +45,7 @@
 
 
 def chunks_of(levels):
-    sizes = [2] * (levels // 2 - 1) + [1, 1]
+    sizes = [2,2,2,2]
     return [(sum(sizes[:i]), size) for i, size in enumerate(sizes)]
 
 
@@ -248,9 +248,8 @@
 
     for i in range(count):
         to_core(i)
-        if i > 0:
-            along_x(i - 1)
-    along_x(count - 1)
+    for i in range(count):
+        along_x(i)
 
     @pl.when(me == 0)
     def _():

time: 34.4 us -> 33.1 us (0.962)
  Pallas kernels: 33 us -> 31.7 us
    pallas_call x1, Pallas kernels: 31.1 us -> 29.8 us  [fused(): pl.pallas_call(functools.partial(fused_kernel, n, sizes), out_shape=[jax....]
where the time goes in v6:
time: 33.1 us; the launch traced here: 33 us
  Pallas kernels  31.7 us (96%)
  between operations  1.29 us (4%)
    pallas_call x1, Pallas kernels, fused(): pl.pallas_call(functools.partial(fused_kernel, n, sizes), out_shape=[jax....  29.8 us
    pallas_call x1, Pallas kernels, fused(): pl.pallas_call(deliver_kernel, out_shape=[jax.ShapeDtypeStruct(grad.shape...  1.91 us

profile of v6, /device:TPU:0, one launch (start us, length us, event | category | flops | bytes accessed | tf_op | source)
XLA Modules:
  0.0 33.0 jit_solution(5385558346224292922)
XLA Ops:
  1.3 29.8 %fused.1 = (f32[128,1024]{1,0:T(8,128)}, f32[256,128]{1,0:T(8,128)}) custom-call(f32[128,1024]{1,0:T(8,128)} %bitcast.5, f32[4,16,1024]{2,1,0:T(8,128)} %coeffs_hbm.1, s32[16,1024]{1,0:T(8,128)} %dist_hbm.1, s32[128,128]{1,0:T(8,128)} %sources_hbm.1, bf16[128,128,128]{2,1,0:T(8,128)(2,1)} %weights_hbm.1, s32[1,128]{1,0:T(1,128)} %bitcast.8, ...), custom_call_target="tpu_custom_call" | custom-call | tf_op jit(solution)/shard_map/fused/pallas_call | solution.py:368
  31.1 1.9 %deliver.1 = (f32[8,16,1024]{2,1,0:T(8,128)}, f32[32,8,128]{2,1,0:T(8,128)}) custom-call(f32[8,16,1024]{2,1,0:T(8,128)} %bitcast.6, f32[32,8,128]{2,1,0:T(8,128)} %bitcast.7), custom_call_target="tpu_custom_call" | custom-call | tf_op jit(solution)/shard_map/deliver/pallas_call | solution.py:416

commit v7 on v6

--- a/solution.py
+++ b/solution.py
@@ -311,7 +311,7 @@
     def along_z(i):
         x_sent[i].wait()
         quarter[part_of(i)] = half[part_of(i), my_x] + got_x[part_of(i)]
-        for k in range(1, nz):
+        for k in [2, 1, 3]:
             z_sent.append(
                 pltpu.make_async_remote_copy(
                     src_ref=quarter.at[part_of(i), lax.rem(my_z + k, nz)],

time: 33.1 us -> 33.5 us (1.012)
  Pallas kernels: 31.7 us -> 32.1 us
    pallas_call x1, Pallas kernels: 29.8 us -> 30.2 us  [fused(): pl.pallas_call(functools.partial(fused_kernel, n, sizes), out_shape=[jax....]
where the time goes in v7:
time: 33.5 us; the launch traced here: 33.4 us
  Pallas kernels  32.1 us (96%)
  between operations  1.29 us (4%)
    pallas_call x1, Pallas kernels, fused(): pl.pallas_call(functools.partial(fused_kernel, n, sizes), out_shape=[jax....  30.2 us
    pallas_call x1, Pallas kernels, fused(): pl.pallas_call(deliver_kernel, out_shape=[jax.ShapeDtypeStruct(grad.shape...  1.91 us

profile of v7, /device:TPU:0, one launch (start us, length us, event | category | flops | bytes accessed | tf_op | source)
XLA Modules:
  0.0 33.4 jit_solution(15895671107028425239)
XLA Ops:
  1.3 30.2 %fused.1 = (f32[128,1024]{1,0:T(8,128)}, f32[256,128]{1,0:T(8,128)}) custom-call(f32[128,1024]{1,0:T(8,128)} %bitcast.5, f32[4,16,1024]{2,1,0:T(8,128)} %coeffs_hbm.1, s32[16,1024]{1,0:T(8,128)} %dist_hbm.1, s32[128,128]{1,0:T(8,128)} %sources_hbm.1, bf16[128,128,128]{2,1,0:T(8,128)(2,1)} %weights_hbm.1, s32[1,128]{1,0:T(1,128)} %bitcast.8, ...), custom_call_target="tpu_custom_call" | custom-call | tf_op jit(solution)/shard_map/fused/pallas_call | solution.py:368
  31.5 1.9 %deliver.1 = (f32[8,16,1024]{2,1,0:T(8,128)}, f32[32,8,128]{2,1,0:T(8,128)}) custom-call(f32[8,16,1024]{2,1,0:T(8,128)} %bitcast.6, f32[32,8,128]{2,1,0:T(8,128)} %bitcast.7), custom_call_target="tpu_custom_call" | custom-call | tf_op jit(solution)/shard_map/deliver/pallas_call | solution.py:416
